TPU v7x, 512 devices: a whole 4x8x8 slice. The times are simulated.
512 devices in a mesh: slab: 8 (over z_hi, core), work: 64 (over x, z_lo, y).
Axes of the slice: x: 4, y: 8, z: 8 (z_hi: 4, z_lo: 2; z = z_hi * 2 + z_lo), core: 2. Of those that a mesh axis runs over, the one named last changes fastest.
Arguments:
- particle_data: bfloat16 [8192, 40960], P(('slab', 'work')), may hold values from -21 to 21
- optics_label: int32 [8192], P(('slab', 'work')), may hold values from 0 to 7
- half_set: int32 [8192], P(('slab', 'work')), may hold values from 0 to 1
- shift_offset: int32 [8192, 2], P(('slab', 'work')), may hold values from -4 to 4
- ctf_bank: float32 [8, 20480], replicated, may hold values from -1 to 1
- noise_power: float32 [20480], replicated, may hold values from 2 to 20
- half_maps: bfloat16 [2, 256, 40960], P(None, 'slab', 'work'), may hold values from -6 to 6
- orient_index: int32 [8], replicated, may hold values from 0 to 4607
Outputs:
- log_total: float32 [8192], P(('slab', 'work'))
- volume_update: float32 [2, 256, 40960], P(None, 'slab', 'work')
All inputs are finite; a program needn't handle non-finite values.
Results may differ from a plain program's by a relative error of at most 0.007.
The roundings to bfloat16 on the way count: a program that leaves them out, or rounds other values in their place, can miss the bound.
Values may be sent and summed in bfloat16 or wider, within the bound.
A program may use at most 64 MiB of HBM per device.

v0:
```python
import math

import jax
import jax.numpy as jnp
from jax import lax
from jax.sharding import PartitionSpec as P

ORDER = 256
PIX = 20480
GRID = 4608


def pixel_coords():
    pixel = lax.iota(jnp.int32, PIX)
    coord_u = (pixel // ORDER).astype(jnp.float32)
    coord_v = (pixel % ORDER - ORDER // 2).astype(jnp.float32)
    return (coord_u, coord_v)


def sines_of(indices):
    theta = math.pi * (indices.astype(jnp.float32) + 0.5) / GRID - 0.5 * math.pi
    return jnp.sin(theta)


def column_tent(orient_sines, planes, col_ids):
    pixel = col_ids % PIX
    coord_v = (pixel % ORDER - ORDER // 2).astype(jnp.float32)
    depth = ORDER // 2 + orient_sines[:, None] * coord_v[None, :]
    return jnp.maximum(0.0, 1.0 - jnp.abs(planes[None, :, None] - depth[:, None, :]))


def body(
    particle_data,
    optics_label,
    half_set,
    shift_offset,
    ctf_bank,
    noise_power,
    half_maps,
    orient_index,
):
    plane_count = half_maps.shape[1]
    col_count = half_maps.shape[2]
    group_count = ctf_bank.shape[0]
    orient_count = orient_index.shape[0]
    onehot = (optics_label[:, None] == lax.iota(jnp.int32, group_count)[None, :]).astype(
        jnp.float32
    )
    ctf_rows = jnp.dot(onehot, ctf_bank, precision=lax.Precision.HIGHEST)
    coord_u, coord_v = pixel_coords()
    shift_x = shift_offset[:, 0:1].astype(jnp.float32)
    shift_y = shift_offset[:, 1:2].astype(jnp.float32)
    phase_angle = -2.0 * math.pi * (coord_u[None, :] * shift_x + coord_v[None, :] * shift_y) / ORDER
    cosine = jnp.cos(phase_angle)
    sine_part = jnp.sin(phase_angle)
    values = particle_data.astype(jnp.float32)
    real_part = values[:, :PIX]
    imag_part = values[:, PIX:]
    factor = ctf_rows / noise_power[None, :]
    prepared = jnp.concatenate(
        [
            (real_part * cosine - imag_part * sine_part) * factor,
            (real_part * sine_part + imag_part * cosine) * factor,
        ],
        axis=1,
    ).astype(jnp.bfloat16)
    ctf_square = ctf_bank * ctf_bank / noise_power[None, :]
    ctf_twice = jnp.concatenate([ctf_square, ctf_square], axis=1)
    planes = (lax.axis_index("slab") * plane_count + lax.iota(jnp.int32, plane_count)).astype(
        jnp.float32
    )
    col_ids = lax.axis_index("work") * col_count + lax.iota(jnp.int32, col_count)
    orient_sines = sines_of(orient_index)
    tent_table = column_tent(orient_sines, planes, col_ids)
    partial_value = jnp.einsum(
        "ozc,hzc->hoc", tent_table, half_maps.astype(jnp.float32), precision=lax.Precision.HIGHEST
    )
    slices = lax.psum(partial_value, "slab").astype(jnp.bfloat16)
    shard_piece = lax.all_gather(slices, "work", axis=2, tiled=True)
    cross_list = []
    power_list = []
    for half_index in range(2):
        slice_rows = shard_piece[half_index]
        cross_list.append(jnp.dot(prepared, slice_rows.T, preferred_element_type=jnp.float32))
        slice_float = slice_rows.astype(jnp.float32)
        power_list.append(
            jnp.dot(ctf_twice, (slice_float * slice_float).T, precision=lax.Precision.HIGHEST)
        )
    cross_terms = jnp.stack(cross_list)
    power_table = jnp.stack(power_list)
    first_mask = half_set[:, None] == 0
    picked_first = jnp.dot(onehot, power_table[0], precision=lax.Precision.HIGHEST)
    picked_second = jnp.dot(onehot, power_table[1], precision=lax.Precision.HIGHEST)
    logits = jnp.where(
        first_mask, cross_terms[0] - 0.5 * picked_first, cross_terms[1] - 0.5 * picked_second
    )
    highest = jnp.max(logits, axis=1, keepdims=True)
    summed = jnp.sum(jnp.exp(logits - highest), axis=1, keepdims=True)
    log_total = highest + jnp.log(summed)
    weights = jnp.exp(logits - log_total).astype(jnp.bfloat16)
    zero_weight = jnp.zeros_like(weights)
    both_weights = jnp.concatenate(
        [
            jnp.where(first_mask, weights, zero_weight),
            jnp.where(half_set[:, None] == 1, weights, zero_weight),
        ],
        axis=1,
    )
    work_sums = lax.psum_scatter(
        lax.dot_general(
            prepared, both_weights, (((0,), (0,)), ((), ())), preferred_element_type=jnp.float32
        ),
        "work",
        scatter_dimension=0,
        tiled=True,
    )
    own_sums = lax.psum(work_sums, "slab")
    grouped_sums = own_sums.reshape(col_count, 2, orient_count)
    volume_update = jnp.einsum(
        "ozc,cho->hzc", tent_table, grouped_sums, precision=lax.Precision.HIGHEST
    )
    return (log_total[:, 0], volume_update)


def solution(mesh):
    placed = (
        P(("slab", "work"), None),
        P(("slab", "work")),
        P(("slab", "work")),
        P(("slab", "work"), None),
        P(),
        P(),
        P(None, "slab", "work"),
        P(),
    )
    return jax.shard_map(
        body,
        mesh=mesh,
        in_specs=placed,
        out_specs=(P(("slab", "work")), P(None, "slab", "work")),
        check_vma=False,
    )
```

profile of v0, /device:TPU:1, one launch (start us, length us, event | category | flops | bytes accessed | tf_op | source)
XLA Modules:
  0.0 722.0 jit_solution(6034795557249571493)
XLA Ops:
  7.2 0.0 all-gather.2.cloned.1.call-start
  7.2 0.7 add_sine_fusion
  7.9 0.1 multiply_add_fusion
  8.0 0.2 copy.22
  8.2 1.1 copy.23
  9.3 0.0 copy-start.3
  9.3 0.0 copy-start
  9.3 2.8 fusion.1
  12.1 0.2 copy.24
  12.3 33.5 %psum.14 = bf16[2,8,640]{2,1,0:T(8,128)(2,1)} all-reduce(f32[2,8,640]{2,1,0:T(8,128)S(1)} %bitcast.25), channel_id=1, replica_groups=mesh['slab'=8,'work'=64] {'slab'}, use_global_device_ids=true, to_apply=%region_0.1 | all-reduce | flops 10240 | bytes 61440 | tf_op jit(solution)/shard_map/psum | solution.py:78
  45.9 0.0 all-gather.2.cloned.1.call-update
  45.9 0.0 reduce-scatter.2.cloned.1.call-start
  46.0 0.0 copy-done.3
  46.0 0.0 copy-done
  46.0 0.0 copy-start.6
  46.0 0.0 copy-start.1
  46.0 0.0 copy-start.2
  46.0 0.0 copy-start.7
  46.0 0.2 convert_element_type.55
  46.2 0.4 copy-done.6
  46.7 0.4 copy-done.1
  47.1 0.0 copy-done.2
  47.1 0.0 copy-done.7
  47.1 6.2 multiply_convert_fusion.1
  53.3 0.1 multiply_divide_fusion
  53.4 249.8 %all-gather.2.cloned.1.call-done = bf16[2,8,40960]{2,1,0:T(8,128)(2,1)} async-done(((bf16[2,8,640]{2,1,0:T(8,128)(2,1)}), bf16[2,8,40960]{2,1,0:T(8,128)(2,1)}) %all-gather.2.cloned.1.call-update) | async-done | bytes 1310736 | tf_op jit(solution)/shard_map/all_gather | solution.py:79
  303.2 0.0 copy-start.5
  303.2 3.9 fusion.2
  307.1 0.0 copy-done.5
  307.1 0.6 fusion.23
  307.7 0.2 fusion.19
  307.9 0.6 fusion.22
  308.6 3.0 fusion.3
  311.5 0.2 fusion.56
  311.8 0.0 copy-start.4
  311.9 2.0 fusion.24
  313.8 0.0 copy-done.4
  313.8 0.0 reduce-scatter.2.cloned.1.call-update
  313.9 313.2 %reduce-scatter.2.cloned.1.call-done = f32[640,16]{0,1:T(8,128)} async-done(((f32[40960,16]{0,1:T(8,128)}), f32[640,16]{0,1:T(8,128)}) %reduce-scatter.2.cloned.1.call-update) | async-done | bytes 40976 | tf_op jit(solution)/shard_map/reduce_scatter | solution.py:109
  627.1 1.1 copy.25
  628.1 81.5 %psum.15 = f32[640,2,8]{2,1,0:T(2,128)S(1)} all-reduce(f32[640,2,8]{2,1,0:T(2,128)S(1)} %copy.25), channel_id=1, replica_groups=mesh['slab'=8,'work'=64] {'slab'}, use_global_device_ids=true, to_apply=%region_4.5 | all-reduce | flops 10240 | bytes 81920 | tf_op jit(solution)/shard_map/psum | solution.py:117
  709.6 4.7 fusion.18
  714.3 0.9 copy.26
  (8 shorter events, 0.1 us)
Async XLA Ops:
  7.2 296.0 %all-gather.2.cloned.1.call-start = ((), (), s32[]{:S(2)}) async-start(), calls=%async_computation.1 | async-start | bytes 1331200 | tf_op jit(solution)/shard_map/all_gather | solution.py:79
  9.3 36.7 %copy-start.3 = (s32[16,2]{0,1:T(2,128)S(1)}, s32[16,2]{0,1:T(2,128)}, u32[]{:S(2)}) copy-start(s32[16,2]{0,1:T(2,128)} %param.11) | copy-start | bytes 388
  9.3 36.7 %copy-start = (bf16[16,40960]{1,0:T(8,128)(2,1)S(1)}, bf16[16,40960]{1,0:T(8,128)(2,1)}, u32[]{:S(2)}) copy-start(bf16[16,40960]{1,0:T(8,128)(2,1)} %param.8) | copy-start | bytes 3932164
  45.9 581.2 %reduce-scatter.2.cloned.1.call-start = ((), (), s32[]{:S(2)}) async-start(), calls=%async_computation.2 | async-start | bytes 2662400 | tf_op jit(solution)/shard_map/reduce_scatter | solution.py:109
  46.0 0.7 copy-start.6
  46.0 1.1 copy-start.1
  46.0 1.1 copy-start.2
  46.0 1.1 copy-start.7
  303.2 4.0 copy-start.5
  311.8 2.0 copy-start.4
Sparse Core Ops, SparseCore 0:
  46.0 257.1 all-gather.1
  314.0 313.0 reduce-scatter.1
where the time goes:
time: 722 us
  waiting for transfers between devices  563 us (78%)
  blocking collectives  115 us (16%)
  matrix products  24.2 us (3%)
  between operations  14.2 us (2%)
    reduce_scatter x1, waiting for transfers between devices, body(): lax.psum_scatter(lax.dot_general(prepared, both_weights, (((0,), (0,)), (...  313 us
    all_gather x1, waiting for transfers between devices, body(): shard_piece = lax.all_gather(slices, 'work', axis=2, tiled=True)  250 us
    psum x1, blocking collectives, body(): own_sums = lax.psum(work_sums, 'slab')  81.5 us
    psum x1, blocking collectives, body(): slices = lax.psum(partial_value, 'slab').astype(jnp.bfloat16)  33.5 us
  transfers between devices with their start and end apart: 2, of which 2 were waited for; matrix products, arithmetic and copies ran while one was open for 1% of the time, Pallas kernels for 0%

commit v1 on v0

v1 whole, which is shorter than its diff:
```python
import math

import jax
import jax.numpy as jnp
from jax import lax
from jax.experimental import pallas as pl
from jax.experimental.pallas import tpu as pltpu
from jax.sharding import PartitionSpec as P

ORDER = 256
PIX = 20480
GRID = 4608
GROUPS = 8
ORIENTS = 8
NX, NY, NZ = 4, 8, 8
PLANES = 32
BLOCK = 640
CHUNK = NY * BLOCK
ROWS = 2 * ORIENTS
MINE = 16
PAIR = 2 * MINE
LANES = 128
TILES = BLOCK // LANES
MESH = pl.DeviceIdType.MESH
F32 = jnp.float32
BF16 = jnp.bfloat16


def device(x, y, z, core):
    return {
        "slab": lax.div(z, 2) * 2 + core,
        "work": (x * 2 + lax.rem(z, 2)) * NY + y,
    }


def turn_of(steps):
    k = lax.bitwise_and(steps, 255)
    quadrant = lax.shift_right_logical(k + 32, 6)
    r = (k - 64 * quadrant).astype(F32) * F32(2.0 * math.pi / ORDER)
    r2 = r * r
    s = r * (1.0 + r2 * (-1.0 / 6 + r2 * (1.0 / 120 + r2 * (-1.0 / 5040 + r2 * (1.0 / 362880)))))
    c = 1.0 + r2 * (-0.5 + r2 * (1.0 / 24 + r2 * (-1.0 / 720 + r2 * (1.0 / 40320 - r2 * (1.0 / 3628800)))))
    odd = lax.bitwise_and(quadrant, 1) == 1
    low = jnp.where(odd, s, c)
    high = jnp.where(odd, c, s)
    turned = lax.bitwise_and(quadrant, 3)
    cosine = jnp.where((turned == 1) | (turned == 2), -low, low)
    sine = jnp.where(turned >= 2, -high, high)
    return cosine, -sine


def kernel(
    orient, label, half, shift, maps, data, ctf, noise,
    log_out, volume_out,
    tent, part, swap, own_half, z_in, slices, raw, meta, ctf_v, noise_v, square, turn_u, turn_v,
    prep, pad, mass, logit, other_logit, weight, x_out, x_in, own, y_out, y_in, z_out, total_in, total,
    local_sem, core_send, core_recv, raw_send, raw_recv, zs, zr, ag_ys, ag_xs, ag_r, xs, xr, ys, yr, ts, tr,
):
    slab = lax.axis_index("slab")
    work = lax.axis_index("work")
    core = lax.rem(slab, 2)
    zh = lax.div(slab, 2)
    x = lax.div(work, 2 * NY)
    zl = lax.rem(lax.div(work, NY), 2)
    y = lax.rem(work, NY)
    z = 2 * zh + zl
    far = 1 - core
    partner = device(x, y, z, far)

    def remote(src, dst, send, recv, target):
        return pltpu.make_async_remote_copy(
            src_ref=src, dst_ref=dst, send_sem=send, recv_sem=recv, device_id=target, device_id_type=MESH
        )

    def arrived(dst, recv):
        remote(dst, dst, recv, recv, partner).wait_recv()

    def left(src, send):
        remote(src, src, send, send, partner).wait_send()

    barrier = pltpu.get_barrier_semaphore()
    friends = [partner]
    friends += [device(x, y, lax.rem(z + d, NZ), k) for d in range(1, NZ) for k in range(2)]
    friends += [device(x, lax.rem(y + d, NY), z, core) for d in range(1, NY)]
    friends += [device(lax.rem(x + d, NX), y, z, core) for d in range(1, NX)]
    for friend in friends:
        pl.semaphore_signal(barrier, inc=1, device_id=friend, device_id_type=MESH)

    def columns(q, k):
        return pl.ds(pl.multiple_of(q * (2 * CHUNK) + k * CHUNK, LANES), CHUNK)

    local = [
        pltpu.make_async_copy(data.at[:, columns(q, core)], raw.at[core, q], local_sem.at[q]) for q in range(4)
    ]
    for q in range(2):
        local.append(pltpu.make_async_copy(ctf.at[:, columns(q, core)], ctf_v.at[q], local_sem.at[4 + q]))
        local.append(pltpu.make_async_copy(noise.at[:, columns(q, core)], noise_v.at[q], local_sem.at[6 + q]))
    for copy in local:
        copy.start()

    row8 = lax.broadcasted_iota(jnp.int32, (ORIENTS, LANES), 0)
    lane8 = lax.broadcasted_iota(jnp.int32, (ORIENTS, LANES), 1)
    index = jnp.zeros((ORIENTS, LANES), jnp.int32)
    for o in range(ORIENTS):
        index = jnp.where(row8 == o, orient[o], index)
    sines = jnp.sin(math.pi * (index.astype(F32) + 0.5) / GRID - 0.5 * math.pi)
    plane = (slab * PLANES + lax.broadcasted_iota(jnp.int32, (PLANES, LANES), 0)).astype(F32)
    lane1 = lax.broadcasted_iota(jnp.int32, (1, LANES), 1)
    for t in range(TILES):
        tile = slice(t * LANES, (t + 1) * LANES)
        coord_v = (lane1 - LANES + LANES * lax.rem(work + t, 2)).astype(F32)
        values = [maps[h, :, tile].astype(F32) for h in range(2)]
        found = [[], []]
        for o in range(ORIENTS):
            depth = ORDER // 2 + sines[o : o + 1, :] * coord_v
            near = jnp.maximum(0.0, 1.0 - jnp.abs(plane - depth))
            tent[o, :, tile] = near
            for h in range(2):
                found[h].append(jnp.sum(near * values[h], axis=0, keepdims=True))
        for h in range(2):
            part[h, :, tile] = jnp.concatenate(found[h], axis=0)

    row16 = lax.broadcasted_iota(jnp.int32, (MINE, LANES), 0)
    about = [jnp.zeros((MINE, LANES), jnp.int32) for _ in range(3)]
    across = jnp.zeros((ORIENTS, LANES), jnp.int32)
    for i in range(MINE):
        here = row16 == i
        about[0] = jnp.where(here, label[i], about[0])
        about[1] = jnp.where(here, shift[i, 0], about[1])
        about[2] = jnp.where(here, shift[i, 1], about[2])
        there = lane8 == core * MINE + i
        across = jnp.where(there & (row8 == 0), label[i], across)
        across = jnp.where(there & (row8 == 1), half[i], across)
    for j in range(3):
        meta[core, j] = about[j]
    meta[core, 3, 0:8, :] = across
    meta[core, 3, 8:16, :] = across

    pl.semaphore_wait(barrier, len(friends))

    swap_copy = remote(part.at[far], swap, core_send.at[0], core_recv.at[0], partner)
    swap_copy.start()
    meta_copy = remote(meta.at[core], meta.at[core], core_send.at[1], core_recv.at[1], partner)
    meta_copy.start()
    raw_copies = [
        remote(data.at[:, columns(q, far)], raw.at[core, q], raw_send.at[q], raw_recv.at[q], partner)
        for q in range(4)
    ]
    for copy in raw_copies:
        copy.start()

    swap_copy.wait_recv()
    own_half[...] = part[core] + swap[...]
    z_copies = [
        remote(own_half, z_in.at[slab], zs.at[d], zr.at[slab], device(x, y, lax.rem(z + d, NZ), zl))
        for d in range(NZ)
    ]
    for copy in z_copies[1:]:
        copy.start()

    @pl.when(core == zl)
    def _():
        z_in[slab] = own_half[...]

    @pl.when(core != zl)
    def _():
        z_copies[0].start()

    for copy in local:
        copy.wait()
    arrived(meta.at[far], core_recv.at[1])
    for q in range(4):
        arrived(raw.at[far, q], raw_recv.at[q])

    label32 = jnp.concatenate([meta[0, 0], meta[1, 0]], axis=0)
    move_u = jnp.concatenate([meta[0, 1], meta[1, 1]], axis=0)
    move_v = jnp.concatenate([meta[0, 2], meta[1, 2]], axis=0)
    lane32 = lax.broadcasted_iota(jnp.int32, (PAIR, LANES), 1)
    for v in range(2):
        cosine, sine = turn_of((lane32 + (v - 1) * LANES) * move_v)
        turn_v[v, 0] = cosine
        turn_v[v, 1] = sine
    per_chunk = CHUNK // ORDER
    coord_u = lane32 + core * per_chunk + jnp.where(lane32 >= per_chunk, per_chunk, 0)
    cosine, sine = turn_of(coord_u * move_u)
    for t in range(2 * per_chunk):
        turn_u[t, 0] = jnp.broadcast_to(cosine[:, t : t + 1], (PAIR, LANES))
        turn_u[t, 1] = jnp.broadcast_to(sine[:, t : t + 1], (PAIR, LANES))
    bits = [lax.bitwise_and(label32, 1 << j) != 0 for j in range(3)]

    def prepare(step, carry):
        q = lax.div(step, 4)
        pair = lax.rem(step, 4)
        span = pl.ds(pl.multiple_of(pair * (2 * BLOCK), LANES), 2 * BLOCK)
        filters = ctf_v[q, :, span]
        variance = noise_v[q, :, span]
        scaled = filters / variance
        squared = filters * filters / variance
        pieces = [[raw[k, q + 2 * i, :, span] for k in range(2)] for i in range(2)]
        for t in range(2 * TILES):
            tile = slice(t * LANES, (t + 1) * LANES)
            block = pair * 2 + t // TILES
            inside = slice((t % TILES) * LANES, (t % TILES + 1) * LANES)
            square[q * NY + block, :, inside] = squared[:, tile]
            wide = [jnp.broadcast_to(scaled[g : g + 1, tile], (PAIR, LANES)) for g in range(GROUPS)]
            wide = [jnp.where(bits[0], wide[2 * j + 1], wide[2 * j]) for j in range(4)]
            wide = [jnp.where(bits[1], wide[2 * j + 1], wide[2 * j]) for j in range(2)]
            factor = jnp.where(bits[2], wide[1], wide[0])
            u = step * 5 + t // 2
            cos_u, sin_u, cos_v, sin_v = turn_u[u, 0], turn_u[u, 1], turn_v[t % 2, 0], turn_v[t % 2, 1]
            cos_q = cos_u * cos_v - sin_u * sin_v
            sin_q = sin_u * cos_v + cos_u * sin_v
            real, imag = [
                jnp.concatenate([pieces[i][0][:, tile], pieces[i][1][:, tile]], axis=0).astype(F32)
                for i in range(2)
            ]
            prep[q, block, :, inside] = ((real * cos_q - imag * sin_q) * factor).astype(BF16)
            prep[q + 2, block, :, inside] = ((real * sin_q + imag * cos_q) * factor).astype(BF16)
        return carry

    lax.fori_loop(0, 8, prepare, 0)

    for d in range(1, 8):
        s = lax.rem(slab + d, 8)
        arrived(z_in.at[s], zr.at[s])

    @pl.when(core != zl)
    def _():
        arrived(z_in.at[slab], zr.at[slab])

    halves = [z_in[h] + z_in[2 + h] + z_in[4 + h] + z_in[6 + h] for h in range(2)]
    slices[x * NY + y] = jnp.concatenate(halves, axis=0).astype(BF16)

    def block_copy(b, send, target):
        return remote(slices.at[b], slices.at[b], send, ag_r.at[b], target)

    turns = [0, 1, 7, 2, 6, 3, 5, 4]
    for d in (4, 3, 5, 2, 6, 1, 7):
        block_copy(x * NY + y, ag_ys.at[d], device(x, lax.rem(y + d, NY), z, core)).start()
    for d in turns:
        b = x * NY + lax.rem(y + d, NY)
        if d:
            arrived(slices.at[b], ag_r.at[b])
        for e in (2, 1, 3):
            block_copy(b, ag_xs.at[e - 1, d], device(lax.rem(x + e, NX), y, z, core)).start()

    def score(xx, wait):
        def step(j, carry):
            yy = lax.rem(y + lax.rem(lax.div(j + 1, 2) * (1 + 6 * lax.rem(j + 1, 2)), 8), NY)
            b = xx * NY + yy
            if wait:
                arrived(slices.at[b], ag_r.at[b])
            cross, sums = carry
            rows = slices[b]
            cross = cross + lax.dot_general(
                rows, prep[xx, yy], (((1,), (1,)), ((), ())), preferred_element_type=F32
            )
            wide = rows.astype(F32)
            pb = lax.rem(xx, 2) * NY + yy
            sums = list(sums)
            for t in range(TILES):
                tile = slice(t * LANES, (t + 1) * LANES)
                size = wide[:, tile] * wide[:, tile]
                gain = square[pb, :, tile]
                for g in range(GROUPS):
                    sums[g] = sums[g] + size * gain[g : g + 1, :]
            return cross, tuple(sums)

        return step

    carry = (jnp.zeros((ROWS, PAIR), F32), tuple(jnp.zeros((ROWS, LANES), F32) for _ in range(GROUPS)))
    for e in (0, 1, 3, 2):
        carry = lax.fori_loop(0, NY, score(lax.rem(x + e, NX), e > 0), carry)
    cross, sums = carry

    about_lanes = meta[0, 3] + meta[1, 3]
    label_lane = about_lanes[0:1, :]
    half_lane = about_lanes[1:2, :]
    pad[...] = jnp.zeros((ROWS, LANES), F32)
    pad[:, 0:PAIR] = cross
    value = pad[...]
    for g in range(GROUPS):
        power = jnp.sum(sums[g], axis=1, keepdims=True)
        value = value - jnp.where(label_lane == g, 0.5 * power, 0.0)
    logit[...] = jnp.where(half_lane == 0, value[0:8, :], value[8:16, :])
    logit_copy = remote(logit, other_logit, core_send.at[2], core_recv.at[2], partner)
    logit_copy.start()
    logit_copy.wait_recv()
    logits = logit[...] + other_logit[...]
    highest = jnp.max(logits, axis=0, keepdims=True)
    log_total = highest + jnp.log(jnp.sum(jnp.exp(logits - highest), axis=0, keepdims=True))
    weights = jnp.exp(logits - log_total)
    both = [jnp.where(half_lane == h, weights, 0.0) for h in range(2)]
    weight[...] = jnp.concatenate(both, axis=0).astype(BF16)
    log_out[...] = jnp.where(core == 0, log_total[:, 0:MINE], log_total[:, MINE:PAIR])

    shares = weight[:, 0:PAIR]

    def weighted(xx, yy):
        return jnp.dot(shares, prep[xx, yy], preferred_element_type=F32)

    order = (4, 3, 5, 2, 6, 1, 7, 0)
    for d in order:
        yy = lax.rem(y + d, NY)
        for e in (2, 1, 3):
            xx = lax.rem(x + e, NX)
            x_out[e - 1, d] = weighted(xx, yy).astype(BF16)
            remote(
                x_out.at[e - 1, d], x_in.at[e - 1, d], xs.at[e - 1, d], xr.at[e - 1, d], device(xx, y, z, core)
            ).start()
    for d in order:
        own[d] = weighted(x, lax.rem(y + d, NY))

    for d in order:
        for e in range(3):
            arrived(x_in.at[e, d], xr.at[e, d])
        block = own[d] + x_in[0, d].astype(F32) + x_in[1, d].astype(F32) + x_in[2, d].astype(F32)
        if d:
            y_out[d - 1] = block.astype(BF16)
            remote(
                y_out.at[d - 1], y_in.at[d - 1], ys.at[d - 1], yr.at[d - 1], device(x, lax.rem(y + d, NY), z, core)
            ).start()
    for d in range(7):
        arrived(y_in.at[d], yr.at[d])
        block = block + y_in[d].astype(F32)
    z_out[...] = block

    t_copies = [
        remote(z_out, total_in.at[z], ts.at[d], tr.at[z], device(x, y, 2 * lax.rem(zh + d, 4) + core, core))
        for d in range(4)
    ]
    for copy in t_copies[1:]:
        copy.start()

    @pl.when(core == zl)
    def _():
        total_in[z] = z_out[...]

    @pl.when(core != zl)
    def _():
        t_copies[0].start()

    total_copy = remote(total, total, core_send.at[3], core_recv.at[3], partner)

    @pl.when(core == zl)
    def _():
        for d in range(1, NZ):
            s = lax.rem(z + d, NZ)
            arrived(total_in.at[s], tr.at[s])
        value = total_in[0]
        for s in range(1, NZ):
            value = value + total_in[s]
        total[...] = value
        total_copy.start()

    @pl.when(core != zl)
    def _():
        total_copy.wait_recv()

    for t in range(TILES):
        tile = slice(t * LANES, (t + 1) * LANES)
        rows = total[:, tile]
        for h in range(2):
            value = tent[0, :, tile] * rows[h * 8 : h * 8 + 1, :]
            for o in range(1, ORIENTS):
                value = value + tent[o, :, tile] * rows[h * 8 + o : h * 8 + o + 1, :]
            volume_out[h, :, tile] = value

    left(part.at[far], core_send.at[0])
    left(meta.at[core], core_send.at[1])
    left(logit, core_send.at[2])
    for q in range(4):
        raw_copies[q].wait_send()
    for d in range(1, NZ):
        left(own_half, zs.at[d])
    for d in range(1, NY):
        left(slices.at[x * NY + y], ag_ys.at[d])
    for d in range(NY):
        for e in range(3):
            left(slices.at[x * NY + lax.rem(y + d, NY)], ag_xs.at[e, d])
            left(x_out.at[e, d], xs.at[e, d])
    for d in range(7):
        left(y_out.at[d], ys.at[d])
    for d in range(1, 4):
        left(z_out, ts.at[d])

    @pl.when(core != zl)
    def _():
        left(own_half, zs.at[0])
        left(z_out, ts.at[0])

    @pl.when(core == zl)
    def _():
        left(total, core_send.at[3])


def body(particle_data, optics_label, half_set, shift_offset, ctf_bank, noise_power, half_maps, orient_index):
    dma = pltpu.SemaphoreType.DMA
    smem = pl.BlockSpec(memory_space=pltpu.SMEM)
    vmem = pl.BlockSpec(memory_space=pltpu.VMEM)
    anywhere = pl.BlockSpec(memory_space=pl.ANY)
    log_total, volume = pl.pallas_call(
        kernel,
        out_shape=(
            jax.ShapeDtypeStruct((1, MINE), F32),
            jax.ShapeDtypeStruct((2, PLANES, BLOCK), F32),
        ),
        in_specs=[smem, smem, smem, smem, vmem, anywhere, anywhere, anywhere],
        out_specs=(vmem, vmem),
        scratch_shapes=[
            pltpu.VMEM((ORIENTS, PLANES, BLOCK), F32),
            pltpu.VMEM((2, ORIENTS, BLOCK), F32),
            pltpu.VMEM((ORIENTS, BLOCK), F32),
            pltpu.VMEM((ORIENTS, BLOCK), F32),
            pltpu.VMEM((8, ORIENTS, BLOCK), F32),
            pltpu.VMEM((NX * NY, ROWS, BLOCK), BF16),
            pltpu.VMEM((2, 4, MINE, CHUNK), BF16),
            pltpu.VMEM((2, 4, MINE, LANES), jnp.int32),
            pltpu.VMEM((2, GROUPS, CHUNK), F32),
            pltpu.VMEM((2, 1, CHUNK), F32),
            pltpu.VMEM((2 * NY, GROUPS, BLOCK), F32),
            pltpu.VMEM((40, 2, PAIR, LANES), F32),
            pltpu.VMEM((2, 2, PAIR, LANES), F32),
            pltpu.VMEM((NX, NY, PAIR, BLOCK), BF16),
            pltpu.VMEM((ROWS, LANES), F32),
            pltpu.VMEM((ROWS, LANES), F32),
            pltpu.VMEM((ORIENTS, LANES), F32),
            pltpu.VMEM((ORIENTS, LANES), F32),
            pltpu.VMEM((ROWS, LANES), BF16),
            pltpu.VMEM((3, NY, ROWS, BLOCK), BF16),
            pltpu.VMEM((3, NY, ROWS, BLOCK), BF16),
            pltpu.VMEM((NY, ROWS, BLOCK), F32),
            pltpu.VMEM((7, ROWS, BLOCK), BF16),
            pltpu.VMEM((7, ROWS, BLOCK), BF16),
            pltpu.VMEM((ROWS, BLOCK), F32),
            pltpu.VMEM((NZ, ROWS, BLOCK), F32),
            pltpu.VMEM((ROWS, BLOCK), F32),
            dma((8,)),
            dma((4,)),
            dma((4,)),
            dma((4,)),
            dma((4,)),
            dma((8,)),
            dma((8,)),
            dma((8,)),
            dma((3, 8)),
            dma((NX * NY,)),
            dma((3, 8)),
            dma((3, 8)),
            dma((7,)),
            dma((7,)),
            dma((4,)),
            dma((8,)),
        ],
        compiler_params=pltpu.CompilerParams(
            collective_id=0, has_side_effects=True, vmem_limit_bytes=40 * 1024 * 1024
        ),
        name="score_and_insert",
    )(
        orient_index, optics_label, half_set, shift_offset, half_maps, particle_data, ctf_bank,
        noise_power.reshape(1, PIX),
    )
    return log_total.reshape(MINE), volume


def solution(mesh):
    placed = (
        P(("slab", "work"), None),
        P(("slab", "work")),
        P(("slab", "work")),
        P(("slab", "work"), None),
        P(),
        P(),
        P(None, "slab", "work"),
        P(),
    )
    return jax.shard_map(
        body,
        mesh=mesh,
        in_specs=placed,
        out_specs=(P(("slab", "work")), P(None, "slab", "work")),
        check_vma=False,
    )
```

time: 722 us -> 68.7 us (0.10)
  waiting for transfers between devices: 563 us -> 0 us
  blocking collectives: 115 us -> 0 us
  Pallas kernels: 0 us -> 59.7 us
  matrix products: 24.2 us -> 0 us
  between operations: 14.2 us -> 0.65 us
    reduce_scatter x1 -> x0, waiting for transfers between devices: 313 us -> none  [body(): lax.psum_scatter(lax.dot_general(prepared, both_weights, (((0,), (0,)), (...]
    all_gather x1 -> x0, waiting for transfers between devices: 250 us -> none  [body(): shard_piece = lax.all_gather(slices, 'work', axis=2, tiled=True)]
    psum x2 -> x0, blocking collectives: 115 us -> none  [the longest x1 81.5 us: body(): own_sums = lax.psum(work_sums, 'slab')]
    pallas_call x0 -> x1, Pallas kernels: none -> 59.7 us  [body(): pl.pallas_call(kernel, out_shape=(jax.ShapeDtypeStruct((1, MINE), F32), j...]
    dot_general x10 -> x0, matrix products: 24.2 us -> none  [the longest x2 6.93 us: body(): jnp.dot(ctf_twice, (slice_float * slice_float).T, precision=lax.Precision...]
  transfers between devices with their start and end apart: 2 -> 0, of which waited for: 2 -> 0; matrix products, arithmetic and copies ran while one was open for 1% -> 0% of each run, Pallas kernels for 0% -> 0%
where the time goes in v1:
time: 68.7 us; the launch traced here: 68.4 us
  Pallas kernels  59.7 us (87%)
  local copies, waits for them, and re-layouts  8.07 us (12%)
    pallas_call x1, Pallas kernels, body(): pl.pallas_call(kernel, out_shape=(jax.ShapeDtypeStruct((1, MINE), F32), j...  59.7 us
    unnamed x17, local copies, waits for them, and re-layouts  8.07 us

profile of v1, /device:TPU:1, one launch (start us, length us, event | category | flops | bytes accessed | tf_op | source)
XLA Modules:
  0.0 68.4 jit_solution(14091639425119227253)
XLA Ops:
  0.6 0.8 %copy.10.shift = s32[16,2]{1,0:T(8,128)S(1)} copy(s32[16,2]{0,1:T(2,128)} %param.11) | data formatting | bytes 256 | tf_op args[3]
  1.4 0.0 copy-start
  1.4 1.3 %copy-done = bf16[16,40960]{1,0:T(8,128)(2,1)S(1)} copy-done((bf16[16,40960]{1,0:T(8,128)(2,1)S(1)}, bf16[16,40960]{1,0:T(8,128)(2,1)}, u32[]{:S(2)}) %copy-start) | copy-done | bytes 1310744
  2.7 0.0 copy-start.1
  2.7 1.1 %copy-done.1 = f32[8,20480]{1,0:T(8,128)S(1)} copy-done((f32[8,20480]{1,0:T(8,128)S(1)}, f32[8,20480]{1,0:T(8,128)}, u32[]{:S(2)}) %copy-start.1) | copy-done | bytes 655384
  3.8 0.0 copy-start.2
  3.8 0.9 %copy-done.2 = bf16[2,32,640]{2,1,0:T(8,128)(2,1)S(1)} copy-done((bf16[2,32,640]{2,1,0:T(8,128)(2,1)S(1)}, bf16[2,32,640]{2,1,0:T(8,128)(2,1)}, u32[]{:S(2)}) %copy-start.2) | copy-done | bytes 81944
  4.7 0.0 copy-start.3
  4.7 0.9 %copy-done.3 = f32[20480]{0:T(1024)S(1)} copy-done((f32[20480]{0:T(1024)S(1)}, f32[20480]{0:T(1024)}, u32[]{:S(2)}) %copy-start.3) | copy-done | bytes 81944
  5.6 0.0 copy-start.4
  5.6 0.7 copy-done.4
  6.2 0.0 copy-start.5
  6.2 0.7 copy-done.5
  6.9 0.0 copy-start.6
  6.9 0.7 copy-done.6
  7.5 59.7 %score_and_insert.1 = (f32[1,16]{1,0:T(1,128)S(1)}, f32[2,32,640]{2,1,0:T(8,128)S(1)}) custom-call(s32[8]{0:T(128)S(1)} %copy-done.4, s32[16]{0:T(128)S(1)} %copy-done.5, s32[16]{0:T(128)S(1)} %copy-done.6, s32[16,2]{1,0:T(8,128)S(1)} %copy.10.shift, bf16[2,32,640]{2,1,0:T(8,128)(2,1)S(1)} %copy-done.2, bf16[16,40960]{1,0:T(8,128)(2,1)S(1)} %copy-done, ...), custom_call_target="tpu_custom_call" | custom-call | tf_op jit(solution)/shard_map/score_and_insert/pallas_call | solution.py:402
  67.2 0.5 copy.13
  67.7 0.7 copy.14
Async XLA Ops:
  1.4 1.3 %copy-start = (bf16[16,40960]{1,0:T(8,128)(2,1)S(1)}, bf16[16,40960]{1,0:T(8,128)(2,1)}, u32[]{:S(2)}) copy-start(bf16[16,40960]{1,0:T(8,128)(2,1)} %data.1) | copy-start | bytes 3932164
  2.7 1.1 %copy-start.1 = (f32[8,20480]{1,0:T(8,128)S(1)}, f32[8,20480]{1,0:T(8,128)}, u32[]{:S(2)}) copy-start(f32[8,20480]{1,0:T(8,128)} %ctf.1) | copy-start | bytes 1966084
  3.8 0.9 %copy-start.2 = (bf16[2,32,640]{2,1,0:T(8,128)(2,1)S(1)}, bf16[2,32,640]{2,1,0:T(8,128)(2,1)}, u32[]{:S(2)}) copy-start(bf16[2,32,640]{2,1,0:T(8,128)(2,1)} %maps.1) | copy-start | bytes 245764
  4.7 0.9 %copy-start.3 = (f32[20480]{0:T(1024)S(1)}, f32[20480]{0:T(1024)}, u32[]{:S(2)}) copy-start(f32[20480]{0:T(1024)} %param.13) | copy-start | bytes 245764
  5.6 0.7 copy-start.4
  6.2 0.7 copy-start.5
  6.9 0.7 copy-start.6

commit v2 on v1

v2 whole, which is shorter than its diff:
```python
import math

import jax
import jax.numpy as jnp
from jax import lax
from jax.experimental import pallas as pl
from jax.experimental.pallas import tpu as pltpu
from jax.sharding import PartitionSpec as P

ORDER = 256
PIX = 20480
GRID = 4608
GROUPS = 8
ORIENTS = 8
NX, NY, NZ = 4, 8, 8
PLANES = 32
BLOCK = 640
CHUNK = NY * BLOCK
ROWS = 2 * ORIENTS
MINE = 16
LANES = 128
TILES = BLOCK // LANES
MESH = pl.DeviceIdType.MESH
F32 = jnp.float32
BF16 = jnp.bfloat16


def device(x, y, z, core):
    return {
        "slab": lax.div(z, 2) * 2 + core,
        "work": (x * 2 + lax.rem(z, 2)) * NY + y,
    }


def turn_of(steps):
    k = lax.bitwise_and(steps, 255)
    quadrant = lax.shift_right_logical(k + 32, 6)
    r = (k - 64 * quadrant).astype(F32) * F32(2.0 * math.pi / ORDER)
    r2 = r * r
    s = r * (1.0 + r2 * (-1.0 / 6 + r2 * (1.0 / 120 + r2 * (-1.0 / 5040 + r2 * (1.0 / 362880)))))
    c = 1.0 + r2 * (-0.5 + r2 * (1.0 / 24 + r2 * (-1.0 / 720 + r2 * (1.0 / 40320 - r2 * (1.0 / 3628800)))))
    odd = lax.bitwise_and(quadrant, 1) == 1
    low = jnp.where(odd, s, c)
    high = jnp.where(odd, c, s)
    turned = lax.bitwise_and(quadrant, 3)
    cosine = jnp.where((turned == 1) | (turned == 2), -low, low)
    sine = jnp.where(turned >= 2, -high, high)
    return cosine, -sine


def tents_of(orient, slab, work):
    row = lax.broadcasted_iota(jnp.int32, (ORIENTS, LANES), 0)
    index = jnp.zeros((ORIENTS, LANES), jnp.int32)
    for o in range(ORIENTS):
        index = jnp.where(row == o, orient[o], index)
    sines = jnp.sin(math.pi * (index.astype(F32) + 0.5) / GRID - 0.5 * math.pi)
    plane = (slab * PLANES + lax.broadcasted_iota(jnp.int32, (PLANES, LANES), 0)).astype(F32)
    lane = lax.broadcasted_iota(jnp.int32, (1, LANES), 1)

    def tents(t, o):
        coord_v = (lane - LANES + LANES * lax.rem(work + t, 2)).astype(F32)
        depth = ORDER // 2 + sines[o : o + 1, :] * coord_v
        return jnp.maximum(0.0, 1.0 - jnp.abs(plane - depth))

    return tents


def kernel(
    orient_in, label_in, half_in, shift_in, maps_in, data_in, ctf_in, noise_in,
    log_out, total,
    orient, label, half, shift, maps, data, ctf, noise,
    part, swap, own_half, z_in, slices, meta, square, turn_u, turn_v, staged, prep,
    logit, logit_in, weight, own, y_out, y_in, z_out, total_in,
    local_sem, core_send, core_recv, ms, mr, ps, pr, zs, zr, ag_s, ag_r, ls, lr, ys, yr, ts, tr,
):
    slab = lax.axis_index("slab")
    work = lax.axis_index("work")
    core = lax.rem(slab, 2)
    zh = lax.div(slab, 2)
    x = lax.div(work, 2 * NY)
    zl = lax.rem(lax.div(work, NY), 2)
    y = lax.rem(work, NY)
    z = 2 * zh + zl
    far = 1 - core
    partner = device(x, y, z, far)
    piece = 2 * x + core

    def remote(src, dst, send, recv, target):
        return pltpu.make_async_remote_copy(
            src_ref=src, dst_ref=dst, send_sem=send, recv_sem=recv, device_id=target, device_id_type=MESH
        )

    def arrived(dst, recv):
        remote(dst, dst, recv, recv, partner).wait_recv()

    def left(src, send):
        remote(src, src, send, send, partner).wait_send()

    def along_x(d):
        q = lax.rem(piece + d, 2 * NX)
        return device(lax.div(q, 2), y, z, lax.rem(q, 2))

    barrier = pltpu.get_barrier_semaphore()
    friends = [along_x(d) for d in range(1, 2 * NX)]
    friends += [device(x, y, lax.rem(z + d, NZ), k) for d in range(1, NZ) for k in range(2)]
    friends += [device(x, lax.rem(y + d, NY), z, core) for d in range(1, NY)]
    for friend in friends:
        pl.semaphore_signal(barrier, inc=1, device_id=friend, device_id_type=MESH)

    pairs = [
        (orient_in, orient), (maps_in, maps), (label_in, label), (half_in, half), (shift_in, shift),
        (data_in, data), (ctf_in, ctf), (noise_in, noise),
    ]
    local = [pltpu.make_async_copy(src, dst, local_sem.at[i]) for i, (src, dst) in enumerate(pairs)]
    for copy in local:
        copy.start()

    local[0].wait()
    local[1].wait()
    tents = tents_of(orient, slab, work)
    for t in range(TILES):
        tile = slice(t * LANES, (t + 1) * LANES)
        values = [maps[h, :, tile].astype(F32) for h in range(2)]
        found = [[], []]
        for o in range(ORIENTS):
            near = tents(t, o)
            for h in range(2):
                found[h].append(jnp.sum(near * values[h], axis=0, keepdims=True))
        for h in range(2):
            part[h, :, tile] = jnp.concatenate(found[h], axis=0)

    pl.semaphore_wait(barrier, len(friends))

    swap_copy = remote(part.at[far], swap, core_send.at[0], core_recv.at[0], partner)
    swap_copy.start()

    for copy in local[2:5]:
        copy.wait()
    row8 = lax.broadcasted_iota(jnp.int32, (ORIENTS, LANES), 0)
    lane8 = lax.broadcasted_iota(jnp.int32, (ORIENTS, LANES), 1)
    row16 = lax.broadcasted_iota(jnp.int32, (MINE, LANES), 0)
    lane16 = lax.broadcasted_iota(jnp.int32, (MINE, LANES), 1)
    about = [jnp.zeros((MINE, LANES), jnp.int32) for _ in range(3)]
    across = jnp.zeros((ORIENTS, LANES), jnp.int32)
    for i in range(MINE):
        here = row16 == i
        about[0] = jnp.where(here, label[i], about[0])
        about[1] = jnp.where(here, shift[0, i], about[1])
        about[2] = jnp.where(here, shift[1, i], about[2])
        there = lane8 == piece * MINE + i
        across = jnp.where(there, jnp.where(row8 == 0, label[i], half[i]), across)
    meta[piece] = across
    meta_copies = [remote(meta.at[piece], meta.at[piece], ms.at[d - 1], mr.at[piece], along_x(d)) for d in range(1, 8)]

    for v in range(2):
        cosine, sine = turn_of((lane16 + (v - 1) * LANES) * about[2])
        turn_v[v, 0] = cosine
        turn_v[v, 1] = sine
    cosine, sine = turn_of(lane16 * about[1])
    for u in range(PIX // ORDER):
        turn_u[u, 0] = jnp.broadcast_to(cosine[:, u : u + 1], (MINE, LANES))
        turn_u[u, 1] = jnp.broadcast_to(sine[:, u : u + 1], (MINE, LANES))
    bits = [lax.bitwise_and(about[0], 1 << j) != 0 for j in range(3)]

    swap_copy.wait_recv()
    own_half[...] = part[core] + swap[...]
    z_copies = [
        remote(own_half, z_in.at[slab], zs.at[d], zr.at[slab], device(x, y, lax.rem(z + d, NZ), zl))
        for d in range(NZ)
    ]
    for d in (4, 3, 5, 2, 6, 1, 7):
        z_copies[d].start()

    @pl.when(core == zl)
    def _():
        z_in[slab] = own_half[...]

    @pl.when(core != zl)
    def _():
        z_copies[0].start()

    for copy in local[5:]:
        copy.wait()

    def prepare(q, k, keep):
        def step(pair, carry):
            span = pl.ds(pl.multiple_of(q * (2 * CHUNK) + k * CHUNK + pair * (2 * BLOCK), LANES), 2 * BLOCK)
            imag_span = pl.ds(pl.multiple_of(PIX + q * (2 * CHUNK) + k * CHUNK + pair * (2 * BLOCK), LANES), 2 * BLOCK)
            filters = ctf[:, span]
            variance = noise[:, span]
            scaled = filters / variance
            real_rows = data[:, span]
            imag_rows = data[:, imag_span]
            if keep:
                squared = filters * filters / variance
            for t in range(2 * TILES):
                tile = slice(t * LANES, (t + 1) * LANES)
                if keep:
                    square[pair * 2 + t // TILES, :, (t % TILES) * LANES : (t % TILES + 1) * LANES] = squared[:, tile]
                wide = [jnp.broadcast_to(scaled[g : g + 1, tile], (MINE, LANES)) for g in range(GROUPS)]
                wide = [jnp.where(bits[0], wide[2 * j + 1], wide[2 * j]) for j in range(4)]
                wide = [jnp.where(bits[1], wide[2 * j + 1], wide[2 * j]) for j in range(2)]
                factor = jnp.where(bits[2], wide[1], wide[0])
                u = (2 * q + k) * (CHUNK // ORDER) + pair * 5 + t // 2
                cos_u, sin_u, cos_v, sin_v = turn_u[u, 0], turn_u[u, 1], turn_v[t % 2, 0], turn_v[t % 2, 1]
                cos_q = cos_u * cos_v - sin_u * sin_v
                sin_q = sin_u * cos_v + cos_u * sin_v
                real = real_rows[:, tile].astype(F32)
                imag = imag_rows[:, tile].astype(F32)
                place = pl.ds(pl.multiple_of(pair * (2 * BLOCK) + t * LANES, LANES), LANES)
                staged[2 * q + k, :, place] = ((real * cos_q - imag * sin_q) * factor).astype(BF16)
                staged[2 * (q + 2) + k, :, place] = ((real * sin_q + imag * cos_q) * factor).astype(BF16)
            return carry

        lax.fori_loop(0, NY // 2, step, 0)

    parity = lax.rem(x, 2)

    def part_copy(e, k):
        xx = lax.rem(x + e, NX)
        slot = 2 * e + (0 if k is core else 1)
        return remote(staged.at[2 * xx + k], prep.at[piece], ps.at[slot], pr.at[piece], device(xx, y, z, k))

    for steps, k, dests in (((1, far, (1, 3)), (0, far, (2, 0)), (1, core, (1, 3)), (0, core, (2,)))):
        q = lax.rem(parity + steps, 2)
        prepare(q, k, steps == 0 and k is core)
        for e in dests:
            part_copy(e, k).start()
    keep_copy = pltpu.make_async_copy(staged.at[piece], prep.at[piece], ps.at[0])
    keep_copy.start()
    for copy in meta_copies:
        copy.start()

    for d in range(1, 8):
        s = lax.rem(slab + d, 8)
        arrived(z_in.at[s], zr.at[s])

    @pl.when(core != zl)
    def _():
        arrived(z_in.at[slab], zr.at[slab])

    halves = [z_in[h] + z_in[2 + h] + z_in[4 + h] + z_in[6 + h] for h in range(2)]
    slices[y] = jnp.concatenate(halves, axis=0).astype(BF16)

    for d in (4, 3, 5, 2, 6, 1, 7):
        remote(
            slices.at[y], slices.at[y], ag_s.at[d - 1], ag_r.at[y], device(x, lax.rem(y + d, NY), z, core)
        ).start()

    sums = [jnp.zeros((ROWS, LANES), F32) for _ in range(GROUPS)]
    for d in (0, 1, 7, 2, 6, 3, 5, 4):
        yy = lax.rem(y + d, NY)
        if d:
            arrived(slices.at[yy], ag_r.at[yy])
        for t in range(TILES):
            tile = slice(t * LANES, (t + 1) * LANES)
            rows = slices[yy, :, tile].astype(F32)
            size = rows * rows
            gain = square[yy, :, tile]
            for g in range(GROUPS):
                sums[g] = sums[g] + size * gain[g : g + 1, :]
    for d in range(1, 8):
        p = lax.rem(piece + d, 8)
        arrived(meta.at[p], mr.at[p])
    about_lanes = meta[0]
    for p in range(1, 8):
        about_lanes = about_lanes + meta[p]
    label_lane = about_lanes[0:1, :]
    half_lane = about_lanes[1:2, :]
    penalty = jnp.zeros((ROWS, LANES), F32)
    for g in range(GROUPS):
        power = jnp.sum(sums[g], axis=1, keepdims=True)
        penalty = penalty + jnp.where(label_lane == g, 0.5 * power, 0.0)

    keep_copy.wait()
    for d in range(1, 8):
        p = lax.rem(piece + d, 8)
        arrived(prep.at[p], pr.at[p])
    cross = jnp.zeros((ROWS, LANES), F32)
    for b in range(NY):
        rows = prep[:, :, b * BLOCK : (b + 1) * BLOCK].reshape(LANES, BLOCK)
        cross = cross + lax.dot_general(slices[b], rows, (((1,), (1,)), ((), ())), preferred_element_type=F32)
    value = cross - penalty
    logit[...] = jnp.where(half_lane == 0, value[0:8, :], value[8:16, :])
    for d in range(1, 8):
        remote(logit, logit_in.at[piece], ls.at[d - 1], lr.at[piece], along_x(d)).start()
    logit_in[piece] = logit[...]
    for d in range(1, 8):
        p = lax.rem(piece + d, 8)
        arrived(logit_in.at[p], lr.at[p])
    logits = logit_in[0]
    for p in range(1, 8):
        logits = logits + logit_in[p]
    highest = jnp.max(logits, axis=0, keepdims=True)
    log_total = highest + jnp.log(jnp.sum(jnp.exp(logits - highest), axis=0, keepdims=True))
    weights = jnp.exp(logits - log_total)
    both = [jnp.where(half_lane == h, weights, 0.0) for h in range(2)]
    weight[...] = jnp.concatenate(both, axis=0).astype(BF16)
    shares = weight[...]

    def weighted(yy):
        span = pl.ds(pl.multiple_of(yy * BLOCK, LANES), BLOCK)
        return jnp.dot(shares, prep[:, :, span].reshape(LANES, BLOCK), preferred_element_type=F32)

    for d in (4, 3, 5, 2, 6, 1, 7):
        yy = lax.rem(y + d, NY)
        y_out[d - 1] = weighted(yy).astype(BF16)
        remote(
            y_out.at[d - 1], y_in.at[d - 1], ys.at[d - 1], yr.at[d - 1], device(x, yy, z, core)
        ).start()
    block = weighted(y)
    lane_sets = [log_total[:, p * MINE : (p + 1) * MINE] for p in range(8)]
    chosen = lane_sets[0]
    for p in range(1, 8):
        chosen = jnp.where(piece == p, lane_sets[p], chosen)
    log_out[...] = chosen
    for d in (0, 6, 1, 5, 2, 4, 3):
        arrived(y_in.at[d], yr.at[d])
        block = block + y_in[d].astype(F32)
    own[...] = block
    z_out[...] = block.astype(BF16)

    t_copies = [
        remote(z_out, total_in.at[z], ts.at[d], tr.at[z], device(x, y, 2 * lax.rem(zh + d, 4) + core, core))
        for d in range(4)
    ]
    for d in (2, 1, 3):
        t_copies[d].start()

    @pl.when(core != zl)
    def _():
        t_copies[0].start()

    total_copy = remote(total, total, core_send.at[1], core_recv.at[1], partner)

    @pl.when(core == zl)
    def _():
        value = own[...]
        for d in (1, 7, 2, 6, 3, 5, 4):
            s = lax.rem(z + d, NZ)
            arrived(total_in.at[s], tr.at[s])
            value = value + total_in[s].astype(F32)
        total[...] = value
        total_copy.start()

    @pl.when(core != zl)
    def _():
        total_copy.wait_recv()

    left(part.at[far], core_send.at[0])
    for d in range(7):
        left(meta.at[piece], ms.at[d])
        left(slices.at[y], ag_s.at[d])
        left(logit, ls.at[d])
        left(y_out.at[d], ys.at[d])
        left(own_half, zs.at[d + 1])
        left(staged.at[d], ps.at[d + 1])
    for d in range(1, 4):
        left(z_out, ts.at[d])

    @pl.when(core != zl)
    def _():
        left(own_half, zs.at[0])
        left(z_out, ts.at[0])

    @pl.when(core == zl)
    def _():
        left(total, core_send.at[1])


def insert_kernel(orient, total, log_in, log_out, volume_out):
    tents = tents_of(orient, lax.axis_index("slab"), lax.axis_index("work"))
    log_out[...] = log_in[...]
    for t in range(TILES):
        tile = slice(t * LANES, (t + 1) * LANES)
        rows = total[:, tile]
        found = [jnp.zeros((PLANES, LANES), F32) for _ in range(2)]
        for o in range(ORIENTS):
            near = tents(t, o)
            for h in range(2):
                found[h] = found[h] + near * rows[h * ORIENTS + o : h * ORIENTS + o + 1, :]
        for h in range(2):
            volume_out[h, :, tile] = found[h]


def body(particle_data, optics_label, half_set, shift_offset, ctf_bank, noise_power, half_maps, orient_index):
    dma = pltpu.SemaphoreType.DMA
    smem = pl.BlockSpec(memory_space=pltpu.SMEM)
    vmem = pl.BlockSpec(memory_space=pltpu.VMEM)
    anywhere = pl.BlockSpec(memory_space=pl.ANY)
    log_total, total = pl.pallas_call(
        kernel,
        out_shape=(
            jax.ShapeDtypeStruct((1, MINE), F32),
            jax.ShapeDtypeStruct((ROWS, BLOCK), F32),
        ),
        in_specs=[anywhere] * 8,
        out_specs=(vmem, vmem),
        scratch_shapes=[
            pltpu.SMEM((ORIENTS,), jnp.int32),
            pltpu.SMEM((MINE,), jnp.int32),
            pltpu.SMEM((MINE,), jnp.int32),
            pltpu.SMEM((2, MINE), jnp.int32),
            pltpu.VMEM((2, PLANES, BLOCK), BF16),
            pltpu.VMEM((MINE, 2 * PIX), BF16),
            pltpu.VMEM((GROUPS, PIX), F32),
            pltpu.VMEM((1, PIX), F32),
            pltpu.VMEM((2, ORIENTS, BLOCK), F32),
            pltpu.VMEM((ORIENTS, BLOCK), F32),
            pltpu.VMEM((ORIENTS, BLOCK), F32),
            pltpu.VMEM((8, ORIENTS, BLOCK), F32),
            pltpu.VMEM((NY, ROWS, BLOCK), BF16),
            pltpu.VMEM((8, ORIENTS, LANES), jnp.int32),
            pltpu.VMEM((NY, GROUPS, BLOCK), F32),
            pltpu.VMEM((PIX // ORDER, 2, MINE, LANES), F32),
            pltpu.VMEM((2, 2, MINE, LANES), F32),
            pltpu.VMEM((8, MINE, CHUNK), BF16),
            pltpu.VMEM((8, MINE, CHUNK), BF16),
            pltpu.VMEM((ORIENTS, LANES), F32),
            pltpu.VMEM((8, ORIENTS, LANES), F32),
            pltpu.VMEM((ROWS, LANES), BF16),
            pltpu.VMEM((ROWS, BLOCK), F32),
            pltpu.VMEM((7, ROWS, BLOCK), BF16),
            pltpu.VMEM((7, ROWS, BLOCK), BF16),
            pltpu.VMEM((ROWS, BLOCK), BF16),
            pltpu.VMEM((NZ, ROWS, BLOCK), BF16),
            dma((8,)),
            dma((2,)),
            dma((2,)),
            dma((7,)),
            dma((8,)),
            dma((8,)),
            dma((8,)),
            dma((8,)),
            dma((8,)),
            dma((7,)),
            dma((8,)),
            dma((7,)),
            dma((8,)),
            dma((7,)),
            dma((7,)),
            dma((4,)),
            dma((8,)),
        ],
        compiler_params=pltpu.CompilerParams(
            collective_id=0, has_side_effects=True, vmem_limit_bytes=64 * 1024 * 1024
        ),
        name="score_and_insert",
    )(
        orient_index, optics_label, half_set, shift_offset.T, half_maps, particle_data, ctf_bank,
        noise_power.reshape(1, PIX),
    )
    log_total, volume = pl.pallas_call(
        insert_kernel,
        out_shape=(
            jax.ShapeDtypeStruct((1, MINE), F32),
            jax.ShapeDtypeStruct((2, PLANES, BLOCK), F32),
        ),
        in_specs=[smem, vmem, vmem],
        out_specs=(vmem, vmem),
        name="insert",
    )(orient_index, total, log_total)
    return log_total.reshape(MINE), volume


def solution(mesh):
    placed = (
        P(("slab", "work"), None),
        P(("slab", "work")),
        P(("slab", "work")),
        P(("slab", "work"), None),
        P(),
        P(),
        P(None, "slab", "work"),
        P(),
    )
    return jax.shard_map(
        body,
        mesh=mesh,
        in_specs=placed,
        out_specs=(P(("slab", "work")), P(None, "slab", "work")),
        check_vma=False,
    )
```

time: 68.7 us -> 54.5 us (0.79)
  local copies, waits for them, and re-layouts: 8.07 us -> 0 us
  Pallas kernels: 59.7 us -> 53.6 us
    unnamed x17 -> x0, local copies, waits for them, and re-layouts: 8.07 us -> none
    pallas_call x1, Pallas kernels: 59.7 us -> 52 us  [body(): pl.pallas_call(kernel, out_shape=(jax.ShapeDtypeStruct((1, MINE), F32), j...]
    pallas_call x0 -> x1, Pallas kernels: none -> 1.7 us  [body(): pl.pallas_call(insert_kernel, out_shape=(jax.ShapeDtypeStruct((1, MINE),...]
where the time goes in v2:
time: 54.5 us; the launch traced here: 54.3 us
  Pallas kernels  53.6 us (98%)
  between operations  0.64 us (1%)
    pallas_call x1, Pallas kernels, body(): pl.pallas_call(kernel, out_shape=(jax.ShapeDtypeStruct((1, MINE), F32), j...  52 us
    pallas_call x1, Pallas kernels, body(): pl.pallas_call(insert_kernel, out_shape=(jax.ShapeDtypeStruct((1, MINE),...  1.7 us

profile of v2, /device:TPU:1, one launch (start us, length us, event | category | flops | bytes accessed | tf_op | source)
XLA Modules:
  0.0 54.3 jit_solution(2170201463557407654)
XLA Ops:
  0.6 52.0 %score_and_insert.1 = (f32[1,16]{1,0:T(1,128)}, f32[16,640]{1,0:T(8,128)}) custom-call(s32[8]{0:T(128)} %orient.1, s32[16]{0:T(128)} %label_in.1, s32[16]{0:T(128)} %half_in.1, s32[2,16]{1,0:T(2,128)} %bitcast.4, bf16[2,32,640]{2,1,0:T(8,128)(2,1)} %maps_in.1, bf16[16,40960]{1,0:T(8,128)(2,1)} %data_in.1, f32[8,20480]{1,0:T(8,128)} %ctf_in.1, f32[1,20480]{1,0:T(1,128)} %bitcast.3), custom_call_target="tpu_custom_call" | custom-call | tf_op jit(solution)/shard_map/score_and_insert/pallas_call | solution.py:391
  52.6 1.7 %insert.1 = (f32[1,16]{1,0:T(1,128)}, f32[2,32,640]{2,1,0:T(8,128)}) custom-call(s32[8]{0:T(128)} %orient.1, f32[16,640]{1,0:T(8,128)} %get-tuple-element.6.total, f32[1,16]{1,0:T(1,128)} %get-tuple-element.7.log_in), custom_call_target="tpu_custom_call" | custom-call | tf_op jit(solution)/shard_map/insert/pallas_call | solution.py:453

commit v3 on v2

--- a/solution.py
+++ b/solution.py
@@ -129,11 +129,6 @@
         for h in range(2):
             part[h, :, tile] = jnp.concatenate(found[h], axis=0)
 
-    pl.semaphore_wait(barrier, len(friends))
-
-    swap_copy = remote(part.at[far], swap, core_send.at[0], core_recv.at[0], partner)
-    swap_copy.start()
-
     for copy in local[2:5]:
         copy.wait()
     row8 = lax.broadcasted_iota(jnp.int32, (ORIENTS, LANES), 0)
@@ -161,23 +156,6 @@
         turn_u[u, 0] = jnp.broadcast_to(cosine[:, u : u + 1], (MINE, LANES))
         turn_u[u, 1] = jnp.broadcast_to(sine[:, u : u + 1], (MINE, LANES))
     bits = [lax.bitwise_and(about[0], 1 << j) != 0 for j in range(3)]
-
-    swap_copy.wait_recv()
-    own_half[...] = part[core] + swap[...]
-    z_copies = [
-        remote(own_half, z_in.at[slab], zs.at[d], zr.at[slab], device(x, y, lax.rem(z + d, NZ), zl))
-        for d in range(NZ)
-    ]
-    for d in (4, 3, 5, 2, 6, 1, 7):
-        z_copies[d].start()
-
-    @pl.when(core == zl)
-    def _():
-        z_in[slab] = own_half[...]
-
-    @pl.when(core != zl)
-    def _():
-        z_copies[0].start()
 
     for copy in local[5:]:
         copy.wait()
@@ -221,15 +199,39 @@
         slot = 2 * e + (0 if k is core else 1)
         return remote(staged.at[2 * xx + k], prep.at[piece], ps.at[slot], pr.at[piece], device(xx, y, z, k))
 
-    for steps, k, dests in (((1, far, (1, 3)), (0, far, (2, 0)), (1, core, (1, 3)), (0, core, (2,)))):
-        q = lax.rem(parity + steps, 2)
-        prepare(q, k, steps == 0 and k is core)
-        for e in dests:
+    for steps, k in ((1, far), (0, far), (1, core), (0, core)):
+        prepare(lax.rem(parity + steps, 2), k, steps == 0 and k is core)
+
+    pl.semaphore_wait(barrier, len(friends))
+
+    swap_copy = remote(part.at[far], swap, core_send.at[0], core_recv.at[0], partner)
+    swap_copy.start()
+
+    for k in (far, core):
+        for e in (1, 2, 3):
             part_copy(e, k).start()
+    part_copy(0, far).start()
     keep_copy = pltpu.make_async_copy(staged.at[piece], prep.at[piece], ps.at[0])
     keep_copy.start()
     for copy in meta_copies:
         copy.start()
+
+    swap_copy.wait_recv()
+    own_half[...] = part[core] + swap[...]
+    z_copies = [
+        remote(own_half, z_in.at[slab], zs.at[d], zr.at[slab], device(x, y, lax.rem(z + d, NZ), zl))
+        for d in range(NZ)
+    ]
+    for d in (4, 3, 5, 2, 6, 1, 7):
+        z_copies[d].start()
+
+    @pl.when(core == zl)
+    def _():
+        z_in[slab] = own_half[...]
+
+    @pl.when(core != zl)
+    def _():
+        z_copies[0].start()
 
     for d in range(1, 8):
         s = lax.rem(slab + d, 8)
@@ -321,21 +323,31 @@
     z_out[...] = block.astype(BF16)
 
     t_copies = [
-        remote(z_out, total_in.at[z], ts.at[d], tr.at[z], device(x, y, 2 * lax.rem(zh + d, 4) + core, core))
+        remote(z_out, total_in.at[z], ts.at[d], tr.at[z], device(x, y, 2 * lax.rem(zh + d, 4) + core, 1))
         for d in range(4)
     ]
     for d in (2, 1, 3):
         t_copies[d].start()
-
-    @pl.when(core != zl)
+    stays = (core == zl) & (core == 1)
+
+    @pl.when(~stays)
     def _():
         t_copies[0].start()
 
     total_copy = remote(total, total, core_send.at[1], core_recv.at[1], partner)
 
-    @pl.when(core == zl)
-    def _():
-        value = own[...]
+    @pl.when(core == 1)
+    def _():
+        @pl.when(stays)
+        def _():
+            total[...] = own[...]
+
+        @pl.when(~stays)
+        def _():
+            arrived(total_in.at[z], tr.at[z])
+            total[...] = total_in[z].astype(F32)
+
+        value = total[...]
         for d in (1, 7, 2, 6, 3, 5, 4):
             s = lax.rem(z + d, NZ)
             arrived(total_in.at[s], tr.at[s])
@@ -343,7 +355,7 @@
         total[...] = value
         total_copy.start()
 
-    @pl.when(core != zl)
+    @pl.when(core != 1)
     def _():
         total_copy.wait_recv()
 
@@ -361,9 +373,12 @@
     @pl.when(core != zl)
     def _():
         left(own_half, zs.at[0])
+
+    @pl.when(~stays)
+    def _():
         left(z_out, ts.at[0])
 
-    @pl.when(core == zl)
+    @pl.when(core == 1)
     def _():
         left(total, core_send.at[1])
 

time: 54.5 us -> 52.9 us (0.971)
  Pallas kernels: 53.6 us -> 52.1 us
    pallas_call x1, Pallas kernels: 52 us -> 50.4 us  [body(): pl.pallas_call(kernel, out_shape=(jax.ShapeDtypeStruct((1, MINE), F32), j...]
where the time goes in v3:
time: 52.9 us; the launch traced here: 52.7 us
  Pallas kernels  52.1 us (98%)
  between operations  0.64 us (1%)
    pallas_call x1, Pallas kernels, body(): pl.pallas_call(kernel, out_shape=(jax.ShapeDtypeStruct((1, MINE), F32), j...  50.4 us
    pallas_call x1, Pallas kernels, body(): pl.pallas_call(insert_kernel, out_shape=(jax.ShapeDtypeStruct((1, MINE),...  1.7 us

profile of v3, /device:TPU:1, one launch (start us, length us, event | category | flops | bytes accessed | tf_op | source)
XLA Modules:
  0.0 52.7 jit_solution(10068690833612353854)
XLA Ops:
  0.6 50.4 %score_and_insert.1 = (f32[1,16]{1,0:T(1,128)}, f32[16,640]{1,0:T(8,128)}) custom-call(s32[8]{0:T(128)} %orient.1, s32[16]{0:T(128)} %label_in.1, s32[16]{0:T(128)} %half_in.1, s32[2,16]{1,0:T(2,128)} %bitcast.4, bf16[2,32,640]{2,1,0:T(8,128)(2,1)} %maps_in.1, bf16[16,40960]{1,0:T(8,128)(2,1)} %data_in.1, f32[8,20480]{1,0:T(8,128)} %ctf_in.1, f32[1,20480]{1,0:T(1,128)} %bitcast.3), custom_call_target="tpu_custom_call" | custom-call | tf_op jit(solution)/shard_map/score_and_insert/pallas_call | solution.py:406
  51.0 1.7 %insert.1 = (f32[1,16]{1,0:T(1,128)}, f32[2,32,640]{2,1,0:T(8,128)}) custom-call(s32[8]{0:T(128)} %orient.1, f32[16,640]{1,0:T(8,128)} %get-tuple-element.6.total, f32[1,16]{1,0:T(1,128)} %get-tuple-element.7.log_in), custom_call_target="tpu_custom_call" | custom-call | tf_op jit(solution)/shard_map/insert/pallas_call | solution.py:468

commit v4 on v3

--- a/solution.py
+++ b/solution.py
@@ -199,18 +199,21 @@
         slot = 2 * e + (0 if k is core else 1)
         return remote(staged.at[2 * xx + k], prep.at[piece], ps.at[slot], pr.at[piece], device(xx, y, z, k))
 
-    for steps, k in ((1, far), (0, far), (1, core), (0, core)):
-        prepare(lax.rem(parity + steps, 2), k, steps == 0 and k is core)
-
+    prepare(lax.rem(parity + 1, 2), far, False)
+    prepare(parity, far, False)
     pl.semaphore_wait(barrier, len(friends))
 
     swap_copy = remote(part.at[far], swap, core_send.at[0], core_recv.at[0], partner)
     swap_copy.start()
 
-    for k in (far, core):
-        for e in (1, 2, 3):
-            part_copy(e, k).start()
+    for e in (1, 2, 3):
+        part_copy(e, far).start()
     part_copy(0, far).start()
+
+    prepare(lax.rem(parity + 1, 2), core, False)
+    prepare(parity, core, True)
+    for e in (1, 2, 3):
+        part_copy(e, core).start()
     keep_copy = pltpu.make_async_copy(staged.at[piece], prep.at[piece], ps.at[0])
     keep_copy.start()
     for copy in meta_copies:
@@ -284,7 +287,7 @@
         cross = cross + lax.dot_general(slices[b], rows, (((1,), (1,)), ((), ())), preferred_element_type=F32)
     value = cross - penalty
     logit[...] = jnp.where(half_lane == 0, value[0:8, :], value[8:16, :])
-    for d in range(1, 8):
+    for d in (4, 5, 3, 2, 6, 7, 1):
         remote(logit, logit_in.at[piece], ls.at[d - 1], lr.at[piece], along_x(d)).start()
     logit_in[piece] = logit[...]
     for d in range(1, 8):

time: 52.9 us -> 52.3 us (0.989)
  Pallas kernels: 52.1 us -> 51.5 us
    pallas_call x1, Pallas kernels: 50.4 us -> 49.8 us  [body(): pl.pallas_call(kernel, out_shape=(jax.ShapeDtypeStruct((1, MINE), F32), j...]
where the time goes in v4:
time: 52.3 us; the launch traced here: 52.1 us
  Pallas kernels  51.5 us (98%)
  between operations  0.64 us (1%)
    pallas_call x1, Pallas kernels, body(): pl.pallas_call(kernel, out_shape=(jax.ShapeDtypeStruct((1, MINE), F32), j...  49.8 us
    pallas_call x1, Pallas kernels, body(): pl.pallas_call(insert_kernel, out_shape=(jax.ShapeDtypeStruct((1, MINE),...  1.7 us

profile of v4, /device:TPU:1, one launch (start us, length us, event | category | flops | bytes accessed | tf_op | source)
XLA Modules:
  0.0 52.1 jit_solution(2462791142661996516)
XLA Ops:
  0.6 49.8 %score_and_insert.1 = (f32[1,16]{1,0:T(1,128)}, f32[16,640]{1,0:T(8,128)}) custom-call(s32[8]{0:T(128)} %orient.1, s32[16]{0:T(128)} %label_in.1, s32[16]{0:T(128)} %half_in.1, s32[2,16]{1,0:T(2,128)} %bitcast.4, bf16[2,32,640]{2,1,0:T(8,128)(2,1)} %maps_in.1, bf16[16,40960]{1,0:T(8,128)(2,1)} %data_in.1, f32[8,20480]{1,0:T(8,128)} %ctf_in.1, f32[1,20480]{1,0:T(1,128)} %bitcast.3), custom_call_target="tpu_custom_call" | custom-call | tf_op jit(solution)/shard_map/score_and_insert/pallas_call | solution.py:409
  50.4 1.7 %insert.1 = (f32[1,16]{1,0:T(1,128)}, f32[2,32,640]{2,1,0:T(8,128)}) custom-call(s32[8]{0:T(128)} %orient.1, f32[16,640]{1,0:T(8,128)} %get-tuple-element.6.total, f32[1,16]{1,0:T(1,128)} %get-tuple-element.7.log_in), custom_call_target="tpu_custom_call" | custom-call | tf_op jit(solution)/shard_map/insert/pallas_call | solution.py:471

commit v5 on v4

--- a/solution.py
+++ b/solution.py
@@ -206,13 +206,13 @@
     swap_copy = remote(part.at[far], swap, core_send.at[0], core_recv.at[0], partner)
     swap_copy.start()
 
-    for e in (1, 2, 3):
+    for e in (2, 1, 3):
         part_copy(e, far).start()
     part_copy(0, far).start()
 
     prepare(lax.rem(parity + 1, 2), core, False)
     prepare(parity, core, True)
-    for e in (1, 2, 3):
+    for e in (2, 1, 3):
         part_copy(e, core).start()
     keep_copy = pltpu.make_async_copy(staged.at[piece], prep.at[piece], ps.at[0])
     keep_copy.start()
@@ -386,9 +386,17 @@
         left(total, core_send.at[1])
 
 
-def insert_kernel(orient, total, log_in, log_out, volume_out):
+def insert_kernel(orient_in, total_in, log_in, log_out, volume_out, orient, total, volume, sem, out_sem):
+    copies = [
+        pltpu.make_async_copy(src, dst, sem.at[i])
+        for i, (src, dst) in enumerate(((orient_in, orient), (total_in, total), (log_in, log_out)))
+    ]
+    for copy in copies:
+        copy.start()
+    copies[0].wait()
     tents = tents_of(orient, lax.axis_index("slab"), lax.axis_index("work"))
-    log_out[...] = log_in[...]
+    copies[1].wait()
+    out = []
     for t in range(TILES):
         tile = slice(t * LANES, (t + 1) * LANES)
         rows = total[:, tile]
@@ -398,12 +406,15 @@
             for h in range(2):
                 found[h] = found[h] + near * rows[h * ORIENTS + o : h * ORIENTS + o + 1, :]
         for h in range(2):
-            volume_out[h, :, tile] = found[h]
+            volume[h, :, tile] = found[h]
+        out.append(pltpu.make_async_copy(volume.at[:, :, tile], volume_out.at[:, :, tile], out_sem.at[t]))
+        out[-1].start()
+    for copy in copies[2:] + out:
+        copy.wait()
 
 
 def body(particle_data, optics_label, half_set, shift_offset, ctf_bank, noise_power, half_maps, orient_index):
     dma = pltpu.SemaphoreType.DMA
-    smem = pl.BlockSpec(memory_space=pltpu.SMEM)
     vmem = pl.BlockSpec(memory_space=pltpu.VMEM)
     anywhere = pl.BlockSpec(memory_space=pl.ANY)
     log_total, total = pl.pallas_call(
@@ -474,8 +485,16 @@
             jax.ShapeDtypeStruct((1, MINE), F32),
             jax.ShapeDtypeStruct((2, PLANES, BLOCK), F32),
         ),
-        in_specs=[smem, vmem, vmem],
-        out_specs=(vmem, vmem),
+        in_specs=[anywhere] * 3,
+        out_specs=(anywhere, anywhere),
+        scratch_shapes=[
+            pltpu.SMEM((ORIENTS,), jnp.int32),
+            pltpu.VMEM((ROWS, BLOCK), F32),
+            pltpu.VMEM((2, PLANES, BLOCK), F32),
+            dma((3,)),
+            dma((TILES,)),
+        ],
+        compiler_params=pltpu.CompilerParams(vmem_limit_bytes=64 * 1024 * 1024),
         name="insert",
     )(orient_index, total, log_total)
     return log_total.reshape(MINE), volume

time: 52.3 us -> 52.2 us (level)
  no operation moved by 1% of the time
where the time goes in v5:
time: 52.2 us; the launch traced here: 52 us
  Pallas kernels  51.4 us (98%)
  between operations  0.64 us (1%)
    pallas_call x1, Pallas kernels, body(): pl.pallas_call(kernel, out_shape=(jax.ShapeDtypeStruct((1, MINE), F32), j...  49.7 us
    pallas_call x1, Pallas kernels, body(): pl.pallas_call(insert_kernel, out_shape=(jax.ShapeDtypeStruct((1, MINE),...  1.66 us

profile of v5, /device:TPU:1, one launch (start us, length us, event | category | flops | bytes accessed | tf_op | source)
XLA Modules:
  0.0 52.0 jit_solution(2607361580369130432)
XLA Ops:
  0.6 49.7 %score_and_insert.1 = (f32[1,16]{1,0:T(1,128)}, f32[16,640]{1,0:T(8,128)}) custom-call(s32[8]{0:T(128)} %orient_in.3, s32[16]{0:T(128)} %label_in.1, s32[16]{0:T(128)} %half_in.1, s32[2,16]{1,0:T(2,128)} %bitcast.4, bf16[2,32,640]{2,1,0:T(8,128)(2,1)} %maps_in.1, bf16[16,40960]{1,0:T(8,128)(2,1)} %data_in.1, f32[8,20480]{1,0:T(8,128)} %ctf_in.1, ...), custom_call_target="tpu_custom_call" | custom-call | tf_op jit(solution)/shard_map/score_and_insert/pallas_call | solution.py:420
  50.4 1.7 %insert.1 = (f32[1,16]{1,0:T(1,128)}, f32[2,32,640]{2,1,0:T(8,128)}) custom-call(s32[8]{0:T(128)} %orient_in.3, f32[16,640]{1,0:T(8,128)} %get-tuple-element.6.total_in, f32[1,16]{1,0:T(1,128)} %get-tuple-element.7.log_in), custom_call_target="tpu_custom_call" | custom-call | tf_op jit(solution)/shard_map/insert/pallas_call | solution.py:482
